TPU v7x, 512 devices: a whole 4x4x16 slice. The times are simulated.
512 devices in a mesh: uly: 16 (over y, x), fsdp: 8 (over z_lo, core), rep: 4 (over z_hi).
Axes of the slice: x: 4, y: 4, z: 16 (z_hi: 4, z_lo: 4; z = z_hi * 4 + z_lo), core: 2. Of those that a mesh axis runs over, the one named last changes fastest.
Arguments:
- inputs_norm: bfloat16 [64, 1024, 8192], P(('rep', 'fsdp'), 'uly'), parts along dimension 0, may hold values from -17 to 17
- queries: bfloat16 [64, 1024, 4096], P(('rep', 'fsdp'), 'uly'), parts along dimension 0, may hold values from -8 to 8
- key_states: bfloat16 [64, 1024, 512], P(('rep', 'fsdp'), 'uly'), parts along dimension 0, may hold values from -8 to 8
- value_states: bfloat16 [64, 1024, 512], P(('rep', 'fsdp'), 'uly'), parts along dimension 0, may hold values from -4.5 to 4.5
- context_grad: bfloat16 [64, 1024, 4096], P(('rep', 'fsdp'), 'uly'), parts along dimension 0, may hold values from -17 to 17
Outputs:
- key_weight_grad: bfloat16 [32768, 512], P(('rep', 'uly', 'fsdp')), parts along dimension 0
There are 4 independent parts, one for each index of `rep`. A program takes and returns all parts, laid end to end along the dimension named above; each array names one. Nothing has to cross between parts.
All inputs are finite; a program needn't handle non-finite values. Where the computation divides by a largest or mean magnitude, that divisor is 1e-20 or more.
Results may differ from a plain program's by a relative error of at most 0.029.
Values may be sent and summed in bfloat16 or wider, within the bound.
A program may use at most 128 MiB of HBM per device.

v0:
```python
import math

import jax
import jax.numpy as jnp
from jax import lax
from jax.sharding import PartitionSpec as P

KVH = 4
HD = 128


def local_key_grad(query_rows, key_rows, value_rows, grad_rows):
    seq_len = key_rows.shape[0]
    block_rows = min(512, seq_len)
    score_scale = 1.0 / math.sqrt(HD)
    accumulated = jnp.zeros((seq_len, HD), jnp.float32)
    for block_index in range(seq_len // block_rows):
        first_row = block_index * block_rows
        visible_len = first_row + block_rows
        query_block = query_rows[:, first_row:visible_len]
        grad_block = grad_rows[:, first_row:visible_len]
        key_block = key_rows[:visible_len]
        value_block = value_rows[:visible_len]
        row_pos = first_row + jnp.arange(block_rows)[:, None]
        col_pos = jnp.arange(visible_len)[None, :]
        visible = row_pos >= col_pos
        scores = jnp.where(
            visible,
            jnp.einsum("hbd,ld->hbl", query_block, key_block, preferred_element_type=jnp.float32)
            * score_scale,
            -jnp.inf,
        )
        top_score = jnp.max(scores, axis=-1, keepdims=True)
        total = jnp.sum(jnp.exp(scores - top_score), axis=-1, keepdims=True)
        attn_probs = jnp.exp(scores - top_score) / total
        prob_grad = jnp.einsum(
            "hbd,ld->hbl", grad_block, value_block, preferred_element_type=jnp.float32
        )
        row_terms = jnp.sum(attn_probs * prob_grad, axis=-1, keepdims=True)
        score_grad = (attn_probs * (prob_grad - row_terms) * score_scale).astype(jnp.bfloat16)
        contrib = jnp.einsum(
            "hbl,hbd->ld", score_grad, query_block, preferred_element_type=jnp.float32
        )
        accumulated = accumulated.at[:visible_len].add(contrib)
    return accumulated


def column_term(features, key_all):
    return jnp.einsum("sc,se->ce", features, key_all, preferred_element_type=jnp.float32)


def per_device(inputs_norm, queries, key_states, value_states, context_grad):
    uly_count = lax.axis_size("uly")
    fsdp_count = lax.axis_size("fsdp")
    copies = uly_count // KVH
    seq_here = inputs_norm.shape[0]
    tok_rows = inputs_norm.shape[1]
    seq_len = tok_rows * uly_count
    input_local = jnp.max(jnp.abs(inputs_norm)).astype(jnp.float32)
    key_copies = jnp.repeat(
        key_states.reshape(seq_here, tok_rows, KVH, HD), copies, axis=2
    ).reshape(seq_here, tok_rows, uly_count * HD)
    value_copies = jnp.repeat(
        value_states.reshape(seq_here, tok_rows, KVH, HD), copies, axis=2
    ).reshape(seq_here, tok_rows, uly_count * HD)
    head_query, head_key, head_value, head_grad = (
        lax.all_to_all(queries, "uly", split_axis=2, concat_axis=1, tiled=True),
        lax.all_to_all(key_copies, "uly", split_axis=2, concat_axis=1, tiled=True),
        lax.all_to_all(value_copies, "uly", split_axis=2, concat_axis=1, tiled=True),
        lax.all_to_all(context_grad, "uly", split_axis=2, concat_axis=1, tiled=True),
    )
    heads_here = head_query.shape[2] // HD
    partials = []
    for seq_index in range(seq_here):
        query_heads = head_query[seq_index].reshape(seq_len, heads_here, HD).transpose(1, 0, 2)
        grad_heads = head_grad[seq_index].reshape(seq_len, heads_here, HD).transpose(1, 0, 2)
        partials.append(
            local_key_grad(query_heads, head_key[seq_index], head_value[seq_index], grad_heads)
        )
    partial_value = jnp.stack(partials, axis=0).astype(jnp.bfloat16)
    returned = lax.all_to_all(partial_value, "uly", split_axis=1, concat_axis=2, tiled=True)
    key_grad = jnp.sum(
        returned.astype(jnp.float32).reshape(seq_here, tok_rows, KVH, copies, HD), axis=3
    )
    key_grad = key_grad.astype(jnp.bfloat16).reshape(seq_here, tok_rows, KVH * HD)
    key_local = jnp.max(jnp.abs(key_grad)).astype(jnp.float32)
    input_max, key_max = lax.pmax((input_local, key_local), ("uly", "fsdp"))
    row_width = inputs_norm.shape[2] // (uly_count * fsdp_count)
    features = lax.all_to_all(inputs_norm, "uly", split_axis=2, concat_axis=1, tiled=True).reshape(
        seq_here * seq_len, -1
    )
    key_all = lax.all_gather(key_grad, "uly", axis=1, tiled=True).reshape(
        seq_here * seq_len, KVH * HD
    )
    grad_term = lambda row_start, row_count: column_term(features, key_all)
    raw_grad = lax.psum_scatter(
        grad_term(jnp.int32(0), row_width * lax.axis_size("fsdp")).astype(jnp.bfloat16),
        "fsdp",
        scatter_dimension=0,
        tiled=True,
    ).astype(jnp.float32)
    factor = 36.0 / (input_max * key_max) / math.sqrt(seq_len * seq_here * fsdp_count)
    return (raw_grad * factor).astype(jnp.bfloat16)


def solution(mesh):
    placed = (
        P(("rep", "fsdp"), "uly", None),
        P(("rep", "fsdp"), "uly", None),
        P(("rep", "fsdp"), "uly", None),
        P(("rep", "fsdp"), "uly", None),
        P(("rep", "fsdp"), "uly", None),
    )
    return jax.shard_map(
        per_device,
        mesh=mesh,
        in_specs=placed,
        out_specs=P(("rep", "uly", "fsdp"), None),
        check_vma=False,
    )
```

profile of v0, /device:TPU:1, one launch (start us, length us, event | category | flops | bytes accessed | tf_op | source)
XLA Modules:
  0.0 583.6 jit_solution(13116835084665764341)
XLA Ops:
  6.5 1.1 copy.132
  8.5 1.5 reshape.176
  10.0 7.6 %all-to-all-start.1 = ((bf16[16,2,8192]{2,1,0:T(2,128)(2,1)}), bf16[16,2,8192]{2,1,0:T(2,128)(2,1)S(1)}, u32[]{:S(2)}, u32[]{:S(2)}) async-start(bf16[16,2,8192]{2,1,0:T(2,128)(2,1)} %reshape.176), calls=%async_computation.1 | async-start | bytes 1048576 | tf_op jit(solution)/shard_map/all_to_all | solution.py:68
  18.6 1.5 reshape.180
  20.1 6.5 %all-to-all-done.1 = bf16[16,2,8192]{2,1,0:T(2,128)(2,1)S(1)} async-done(((bf16[16,2,8192]{2,1,0:T(2,128)(2,1)}), bf16[16,2,8192]{2,1,0:T(2,128)(2,1)S(1)}, u32[]{:S(2)}, u32[]{:S(2)}) %all-to-all-start.1) | async-done | bytes 524320 | tf_op jit(solution)/shard_map/all_to_all | solution.py:68
  27.4 3.6 all-to-all-start.3
  31.0 5.0 copy.101
  36.0 2.3 reshape.178
  38.3 1.9 all-to-all-done.3
  41.0 4.7 all-to-all-start
  45.7 5.0 copy.107
  50.8 2.3 reshape.182
  53.8 1.2 iota_compare_fusion
  55.0 3.0 reshape.177
  60.8 6.7 %all-to-all-start.2 = ((bf16[16,2,16384]{2,1,0:T(2,128)(2,1)}), bf16[16,2,16384]{2,1,0:T(2,128)(2,1)}, u32[]{:S(2)}, u32[]{:S(2)}) async-start(bf16[16,2,16384]{2,1,0:T(2,128)(2,1)} %reshape.182), calls=%async_computation.2 | async-start | bytes 2097152 | tf_op jit(solution)/shard_map/all_to_all | solution.py:70
  71.7 1.3 reshape.179
  73.0 1.4 copy.102
  74.5 0.9 fusion.167
  75.5 0.9 copy.152
  76.4 4.2 all-to-all-done.2
  80.6 5.0 reshape.183
  85.6 1.4 copy.108
  87.1 0.9 fusion.166
  89.3 2.6 fusion.99
  92.1 0.9 copy.150
  93.0 1.2 reshape_squeeze.15
  94.2 3.7 fusion.50
  97.9 4.9 fusion.26
  102.8 3.6 fusion.51
  106.4 5.0 fusion.27
  111.4 1.8 fusion.97
  113.1 2.7 fusion.95
  115.8 3.1 fusion.80
  118.9 4.3 fusion.77
  123.2 7.7 %fusion.71 = bf16[1,1024,128]{2,1,0:T(8,128)(2,1)S(1)} fusion(f32[2,512,1024]{2,1,0:T(8,128)} %fusion.26, f32[2,512,1024]{2,1,0:T(8,128)} %fusion.99, f32[512,128]{1,0:T(8,128)S(1)} %fusion.80, bf16[2,1024,128]{2,1,0:T(8,128)(2,1)S(1)} %bitcast.150), kind=kOutput, calls=%fused_computation.62 | convolution fusion | flops 273942528 | bytes 17563648 | tf_op jit(solution)/shard_map/hbl,hbd->ld/dot_general | solution.py:41
  130.9 7.9 %fusion.74 = bf16[1,1024,128]{2,1,0:T(8,128)(2,1)S(1)} fusion(f32[2,512,1024]{2,1,0:T(8,128)} %fusion.27, f32[2,512,1024]{2,1,0:T(8,128)} %fusion.95, f32[512,128]{1,0:T(8,128)S(1)} %fusion.77, bf16[2,1024,128]{2,1,0:T(8,128)(2,1)S(1)} %bitcast.154), kind=kOutput, calls=%fused_computation.63 | convolution fusion | flops 273942528 | bytes 17563648 | tf_op jit(solution)/shard_map/hbl,hbd->ld/dot_general | solution.py:41
  139.4 12.5 %all_to_all.84 = bf16[2,1024,128]{2,0,1:T(2,128)(2,1)S(1)} all-to-all(bf16[2,1024,128]{2,0,1:T(2,128)(2,1)S(1)} %copy.123), channel_id=1, replica_groups=mesh['uly'=16,'fsdp'=8,'rep'=4] {'uly'}, dimensions={1} | all-to-all | bytes 1048576 | tf_op jit(solution)/shard_map/all_to_all | solution.py:81
  153.5 6.9 %copy.126 = bf16[2,64,8192]{1,0,2:T(2,128)(2,1)} copy(bf16[2,64,8192]{2,1,0:T(8,128)(2,1)S(1)} %copy-done) | data formatting | bytes 4194304 | tf_op args[0]
  160.3 7.5 %reshape.184 = bf16[16,2,32768]{2,1,0:T(2,128)(2,1)} reshape(bf16[8192,2,64]{2,1,0:T(2,128)(2,1)} %bitcast.119) | data formatting | bytes 4194304
  167.9 28.3 %all_to_all.85 = bf16[16,2,32768]{2,1,0:T(2,128)(2,1)} all-to-all(bf16[16,2,32768]{2,1,0:T(2,128)(2,1)} %reshape.184), channel_id=1, replica_groups=mesh['uly'=16,'fsdp'=8,'rep'=4] {'uly'}, dimensions={0} | all-to-all | bytes 4194304 | tf_op jit(solution)/shard_map/all_to_all | solution.py:89
  196.2 7.4 %reshape.185 = bf16[8192,2,64]{2,1,0:T(2,128)(2,1)} reshape(bf16[16,2,32768]{2,1,0:T(2,128)(2,1)} %all_to_all.85) | data formatting | bytes 4194304
  203.6 10.6 %copy.138 = bf16[2,64,16,512]{3,1,2,0:T(8,128)(2,1)} copy(bf16[2,64,16,512]{1,0,3,2:T(2,128)(2,1)} %bitcast.118) | data formatting | bytes 4194304 | tf_op jit(solution)/shard_map/all_to_all | solution.py:89
  214.2 14.9 %all-gather.2.cloned.1.call-done = bf16[2,1024,512]{2,1,0:T(8,128)(2,1)} async-done(((bf16[2,64,512]{2,1,0:T(8,128)(2,1)}), bf16[2,1024,512]{2,1,0:T(8,128)(2,1)}) %all-gather.2.cloned.1.call-update) | async-done | bytes 2097168 | tf_op jit(solution)/shard_map/all_gather | solution.py:92
  229.0 3.5 fusion.58
  232.5 1.0 copy.139
  233.5 0.9 abs_reduce_fusion
  235.0 338.8 %all-reduce.2 = (f32[]{:T(128)}, f32[]{:T(128)}) all-reduce(bf16[]{:T(256)} %abs_reduce_fusion, bf16[]{:T(256)} %fusion.133), channel_id=1, replica_groups=mesh['uly'=16,'fsdp'=8,'rep'=4] {'uly','fsdp'}, use_global_device_ids=true, to_apply=%region_15.16 | all-reduce | flops 2 | bytes 12 | tf_op jit(solution)/shard_map/pmax | solution.py:87
  575.2 1.5 multiply_convert_fusion.4
  (58 shorter events, 15.4 us)
Async XLA Ops:
  6.5 11.0 %copy-start.9 = (bf16[2,64,512]{2,1,0:T(8,128)(2,1)S(1)}, bf16[2,64,512]{2,1,0:T(8,128)(2,1)}, u32[]{:S(2)}) copy-start(bf16[2,64,512]{2,1,0:T(8,128)(2,1)} %param.20) | copy-start | bytes 393220
  10.0 16.6 %all-to-all-start.1 = ((bf16[16,2,8192]{2,1,0:T(2,128)(2,1)}), bf16[16,2,8192]{2,1,0:T(2,128)(2,1)S(1)}, u32[]{:S(2)}, u32[]{:S(2)}) async-start(bf16[16,2,8192]{2,1,0:T(2,128)(2,1)} %reshape.176), calls=%async_computation.1 | async-start | bytes 1048576 | tf_op jit(solution)/shard_map/all_to_all | solution.py:68
  26.6 0.8 copy-start.1
  27.4 12.8 %all-to-all-start.3 = ((bf16[16,2,8192]{2,1,0:T(2,128)(2,1)}), bf16[16,2,8192]{2,1,0:T(2,128)(2,1)S(1)}, u32[]{:S(2)}, u32[]{:S(2)}) async-start(bf16[16,2,8192]{2,1,0:T(2,128)(2,1)} %reshape.180), calls=%async_computation.3 | async-start | bytes 1048576 | tf_op jit(solution)/shard_map/all_to_all | solution.py:69
  40.1 0.8 copy-start.2
  41.0 19.9 %all-to-all-start = ((bf16[16,2,16384]{2,1,0:T(2,128)(2,1)}), bf16[16,2,16384]{2,1,0:T(2,128)(2,1)S(1)}, u32[]{:S(2)}, u32[]{:S(2)}) async-start(bf16[16,2,16384]{2,1,0:T(2,128)(2,1)} %reshape.178), calls=%async_computation | async-start | bytes 2097152 | tf_op jit(solution)/shard_map/all_to_all | solution.py:67
  55.0 4.5 copy-start.3
  60.8 19.8 %all-to-all-start.2 = ((bf16[16,2,16384]{2,1,0:T(2,128)(2,1)}), bf16[16,2,16384]{2,1,0:T(2,128)(2,1)}, u32[]{:S(2)}, u32[]{:S(2)}) async-start(bf16[16,2,16384]{2,1,0:T(2,128)(2,1)} %reshape.182), calls=%async_computation.2 | async-start | bytes 2097152 | tf_op jit(solution)/shard_map/all_to_all | solution.py:70
  67.6 161.5 %all-gather.2.cloned.1.call-start = ((), (), s32[]{:S(2)}) async-start(), calls=%async_computation.7 | async-start | bytes 2228224 | tf_op jit(solution)/shard_map/all_gather | solution.py:92
  88.0 0.9 copy-start.6
  88.1 1.2 copy-start.5
  89.3 2.6 copy-start.4
  94.2 3.7 copy-start.7
  115.8 3.1 copy-start.8
  138.8 14.7 %copy-start = (bf16[2,64,8192]{2,1,0:T(8,128)(2,1)S(1)}, bf16[2,64,8192]{2,1,0:T(8,128)(2,1)}, u32[]{:S(2)}) copy-start(bf16[2,64,8192]{2,1,0:T(8,128)(2,1)} %param.17) | copy-start | bytes 6291460
  153.4 421.8 %reduce-scatter.4.cloned.1.call-start = ((), (), s32[]{:S(2)}) async-start(), calls=%async_computation.8 | async-start | bytes 589824 | tf_op jit(solution)/shard_map/reduce_scatter | solution.py:96
Sparse Core Ops, SparseCore 0:
  153.5 75.4 all-gather.1
  233.7 39.4 reduce-scatter.3
where the time goes:
time: 587 us; the launch traced here: 584 us
  blocking collectives  380 us (65%)
  local copies, waits for them, and re-layouts  81.8 us (14%)
  matrix products  51.1 us (9%)
  waiting for transfers between devices  27.5 us (5%)
  starting transfers between devices  22.9 us (4%)
  between operations  15.2 us (3%)
    pmax x1, blocking collectives, per_device(): input_max, key_max = lax.pmax((input_local, key_local), ('uly', 'fsdp'))  339 us
    unnamed x34, local copies, waits for them, and re-layouts  52.8 us
    all_to_all x1, blocking collectives, per_device(): lax.all_to_all(inputs_norm, 'uly', split_axis=2, concat_axis=1, tiled=True)  28.3 us
    dot_general x4, matrix products, local_key_grad(): jnp.einsum('hbl,hbd->ld', score_grad, query_block, preferred_element_type...  23 us
    div x4, matrix products, local_key_grad(): attn_probs = jnp.exp(scores - top_score) / total  17.1 us
    all_gather x1, waiting for transfers between devices, per_device(): lax.all_gather(key_grad, 'uly', axis=1, tiled=True)  14.9 us
    all_to_all x1, blocking collectives, per_device(): lax.all_to_all(partial_value, 'uly', split_axis=1, concat_axis=2, tiled=T...  12.5 us
  transfers between devices with their start and end apart: 6, of which 4 were waited for; matrix products, arithmetic and copies ran while one was open for 12% of the time, Pallas kernels for 0%

commit v1 on v0

v1 whole, which is shorter than its diff:
```python
import math

import jax
import jax.numpy as jnp
from jax import lax
from jax.experimental import pallas as pl
from jax.experimental.pallas import tpu as pltpu
from jax.sharding import PartitionSpec as P

MESH = pl.DeviceIdType.MESH
KVH = 4
HD = 128
SIDE = 4
ULY = SIDE * SIDE
FSDP = 8
SEQ = 2
TOK = 64
GROUP = 8
WIDTH = 8192
BAND = 1024
SLAB = BAND // SIDE
OUT_ROWS = 64
COLS = KVH * HD
SCALE = 1.0 / math.sqrt(HD)
LOG2E = math.log2(math.e)


def kernel(
    x_hbm, q_hbm, k_hbm, v_hbm, g_hbm, out_ref,
    qg, gg, kg, vg, xr, xt, dkacc, part, part_in, dkf, dka, acc,
    y_out, y_in, z_out, z_in, m_own, m_row, m_y_out, m_y_in, m_z_out, m_z_in,
    q_recv, g_recv, kv_recv, x_recv, part_recv, dk_recv, fwd_recv, y_recv, z_recv, m_recv,
    q_send, g_send, kv_send, x_send, part_send, dk_send, fwd_send, y_send, z_send, m_send,
):
    u = lax.axis_index("uly")
    f = lax.axis_index("fsdp")
    y, x = lax.div(u, SIDE), lax.rem(u, SIDE)
    z, c = lax.div(f, 2), lax.rem(f, 2)
    other = 2 * z + 1 - c
    home = lax.div(f, SIDE)

    def to(du, df):
        return {"uly": du, "fsdp": df}

    def remote(src, dst, send, recv, device):
        return pltpu.make_async_remote_copy(
            src_ref=src, dst_ref=dst, send_sem=send, recv_sem=recv,
            device_id=device, device_id_type=MESH,
        )

    def drain(ref, sem):
        pltpu.make_async_copy(ref, ref, sem).wait()

    def ring(offset):
        return lax.rem(u + offset, ULY)

    def row_mate(offset):
        return SIDE * y + lax.rem(x + offset, SIDE)

    def column_mate(offset):
        return SIDE * lax.rem(y + offset, SIDE) + x

    barrier = pltpu.get_barrier_semaphore()

    def greet(device):
        pl.semaphore_signal(barrier, inc=1, device_id=device, device_id_type=MESH)

    for d in range(1, ULY):
        greet(to(ring(d), f))
    for d in range(SIDE):
        greet(to(row_mate(d), other))
    for source_z in range(SIDE):
        source = 2 * source_z + home
        pl.when(source != f)(lambda source=source: greet(to(u, source)))

    for s in range(SEQ):
        cols = pl.ds(pl.multiple_of(y * GROUP * HD, GROUP * HD), GROUP * HD)
        pltpu.make_async_copy(q_hbm.at[s, :, cols], qg.at[s, y], q_recv.at[s]).start()
        pltpu.make_async_copy(g_hbm.at[s, :, cols], gg.at[s, y], g_recv.at[s]).start()
    own_cols = pl.ds(pl.multiple_of(y * HD, HD), HD)
    pltpu.make_async_copy(k_hbm.at[:, :, own_cols], kg.at[:, u], kv_recv.at[0]).start()
    pltpu.make_async_copy(v_hbm.at[:, :, own_cols], vg.at[:, u], kv_recv.at[1]).start()

    def feature_cols(slab, target_x, half):
        start = (slab * SIDE + target_x) * (2 * SLAB) + half * SLAB
        return pl.ds(pl.multiple_of(start, SLAB), SLAB)

    for slab in range(SIDE):
        pltpu.make_async_copy(
            x_hbm.at[:, :, feature_cols(slab, x, c)],
            xr.at[:, 0, x, :, pl.ds(slab * SLAB, SLAB)],
            x_recv,
        ).start()

    pl.semaphore_wait(barrier, ULY - 1 + SIDE + SIDE - jnp.where(home == c, 1, 0))

    def send_heads(s):
        for d in range(1, SIDE):
            target_y = lax.rem(y + d, SIDE)
            cols = pl.ds(pl.multiple_of(target_y * GROUP * HD, GROUP * HD), GROUP * HD)
            device = to(column_mate(d), f)
            remote(q_hbm.at[s, :, cols], qg.at[s, y], q_send.at[s], q_recv.at[s], device).start()
            remote(g_hbm.at[s, :, cols], gg.at[s, y], g_send.at[s], g_recv.at[s], device).start()

    for d in range(1, ULY):
        target = ring(d)
        cols = pl.ds(pl.multiple_of(lax.div(target, SIDE) * HD, HD), HD)
        device = to(target, f)
        remote(k_hbm.at[:, :, cols], kg.at[:, u], kv_send.at[0], kv_recv.at[0], device).start()
        remote(v_hbm.at[:, :, cols], vg.at[:, u], kv_send.at[1], kv_recv.at[1], device).start()
    send_heads(0)
    send_heads(1)
    for dc in range(2):
        for d in range(SIDE):
            if dc == 0 and d == 0:
                continue
            target_x = lax.rem(x + d, SIDE)
            half = c if dc == 0 else 1 - c
            for slab in range(SIDE):
                remote(
                    x_hbm.at[:, :, feature_cols(slab, target_x, half)],
                    xr.at[:, dc, x, :, pl.ds(slab * SLAB, SLAB)],
                    x_send.at[dc], x_recv,
                    to(row_mate(d), f if dc == 0 else other),
                ).start()

    rows = GROUP * TOK
    chunk = SIDE * TOK
    key_at = lax.broadcasted_iota(jnp.int32, (chunk, rows), 0)
    query_at = lax.rem(lax.broadcasted_iota(jnp.int32, (chunk, rows), 1), TOK) + x * TOK
    hidden = key_at > query_at

    def heads_to_rows(block):
        return jnp.concatenate([block[:, h * HD:(h + 1) * HD] for h in range(GROUP)], axis=0)

    def nt(a, b):
        return lax.dot_general(a, b, (((1,), (1,)), ((), ())), preferred_element_type=jnp.float32)

    def attend(s):
        for j in range(SIDE):
            query = heads_to_rows(qg[s, j])
            grad = heads_to_rows(gg[s, j])
            scores = []
            for n in range(j + 1):
                keys = kg[s, SIDE * n:SIDE * (n + 1)].reshape(chunk, HD)
                scores.append(nt(keys, query) * (SCALE * LOG2E))
            scores[j] = jnp.where(hidden, -jnp.inf, scores[j])
            top = jnp.max(scores[0], axis=0, keepdims=True)
            for n in range(1, j + 1):
                top = jnp.maximum(top, jnp.max(scores[n], axis=0, keepdims=True))
            exps = [jnp.exp2(block - top) for block in scores]
            prob_grads = []
            for n in range(j + 1):
                values = vg[s, SIDE * n:SIDE * (n + 1)].reshape(chunk, HD)
                prob_grads.append(nt(values, grad))
            total = sum(jnp.sum(e, axis=0, keepdims=True) for e in exps)
            weighted = sum(
                jnp.sum(e * p, axis=0, keepdims=True) for e, p in zip(exps, prob_grads)
            )
            row_terms = weighted / total
            scale = SCALE / total
            for n in range(j + 1):
                score_grad = (exps[n] * ((prob_grads[n] - row_terms) * scale)).astype(jnp.bfloat16)
                term = jnp.dot(score_grad, query, preferred_element_type=jnp.float32)
                term = term.reshape(SIDE, TOK, HD)
                if n == j:
                    dkacc[s, n] = term
                else:
                    dkacc[s, n] += term

    def send_partials(s):
        for target_x in range(SIDE):
            part[s, target_x] = dkacc[s, :, target_x].astype(jnp.bfloat16)
        for d in range(1, SIDE):
            remote(
                part.at[s, lax.rem(x + d, SIDE)], part_in.at[s, d - 1],
                part_send.at[s], part_recv.at[s], to(row_mate(d), f),
            ).start()

    def send_key_grad(s):
        drain(part_in.at[s], part_recv.at[s])
        summed = dkacc[s, :, x]
        for d in range(SIDE - 1):
            summed += part_in[s, d].astype(jnp.float32)
        dkf[s] = summed.astype(jnp.bfloat16)
        for d in range(1, ULY):
            target = ring(d)
            remote(
                dkf.at[s, lax.div(target, SIDE)],
                dka.at[s, 0, x, :, own_cols],
                dk_send.at[s], dk_recv.at[s], to(target, f),
            ).start()
        pltpu.make_async_copy(
            dkf.at[s, y], dka.at[s, 0, x, :, own_cols], dk_recv.at[s]
        ).start()
        return jnp.max(jnp.abs(summed))

    def forward(s):
        drain(dka.at[s, 0], dk_recv.at[s])
        remote(dka.at[s, 0], dka.at[s, 1], fwd_send.at[s], fwd_recv.at[s], to(u, other)).start()

    def grad_rows(s):
        return dka[s].reshape(2 * SIDE * TOK, COLS)

    for s in range(SEQ):
        drain(qg.at[s], q_recv.at[s])
        drain(gg.at[s], g_recv.at[s])
        if s == 0:
            drain(kg, kv_recv.at[0])
            drain(vg, kv_recv.at[1])
        attend(s)
        send_partials(s)
        if s == 0:
            key_max = send_key_grad(0)

    drain(xr, x_recv)
    input_max = jnp.float32(0.0)
    for s in range(SEQ):
        block = xr[s].reshape(2 * SIDE * TOK, BAND)
        tops = jnp.max(jnp.abs(block), axis=0, keepdims=True).astype(jnp.float32)
        input_max = jnp.maximum(input_max, jnp.max(tops))
        xt[s] = block.T
    forward(0)
    key_max = jnp.maximum(key_max, send_key_grad(1))
    row_at = lax.broadcasted_iota(jnp.int32, (8, HD), 0)
    m_own[...] = jnp.where(row_at < 4, input_max, key_max)
    for dc in range(2):
        for d in range(SIDE):
            if dc or d:
                remote(
                    m_own, m_row.at[dc * SIDE + d - 1], m_send.at[0], m_recv.at[0],
                    to(row_mate(d), f if dc == 0 else other),
                ).start()
    drain(dka.at[0, 1], fwd_recv.at[0])
    acc[...] = jnp.dot(xt[0], grad_rows(0), preferred_element_type=jnp.float32)
    forward(1)
    drain(m_row, m_recv.at[0])
    m_y_out[...] = jnp.maximum(m_own[...], jnp.max(m_row[...], axis=0))
    for d in range(1, SIDE):
        remote(
            m_y_out, m_y_in.at[d - 1], m_send.at[1], m_recv.at[1], to(column_mate(d), f)
        ).start()
    drain(dka.at[1, 1], fwd_recv.at[1])

    def slab_grad(target_y):
        at = pl.ds(pl.multiple_of(target_y * SLAB, SLAB), SLAB)
        return acc[at] + jnp.dot(xt[1, at], grad_rows(1), preferred_element_type=jnp.float32)

    for d in range(1, SIDE):
        y_out[d - 1] = slab_grad(lax.rem(y + d, SIDE)).astype(jnp.bfloat16)
        remote(
            y_out.at[d - 1], y_in.at[d - 1], y_send.at[d - 1], y_recv.at[d - 1],
            to(column_mate(d), f),
        ).start()
    slab_sum = slab_grad(y)
    drain(m_y_in, m_recv.at[1])
    m_z_out[...] = jnp.maximum(m_y_out[...], jnp.max(m_y_in[...], axis=0))
    for d in range(1, SIDE):
        drain(y_in.at[d - 1], y_recv.at[d - 1])
        slab_sum += y_in[d - 1].astype(jnp.float32)
    z_out[...] = slab_sum.reshape(SIDE, OUT_ROWS, COLS).astype(jnp.bfloat16)
    for k in range(SIDE):
        target = SIDE * c + k

        def away(k=k, target=target):
            remote(z_out.at[k], z_in.at[z], z_send.at[0], z_recv, to(u, target)).start()
            remote(m_z_out, m_z_in.at[z], m_send.at[2], m_recv.at[2], to(u, target)).start()

        def stay(k=k):
            pltpu.make_async_copy(z_out.at[k], z_in.at[z], z_recv).start()
            pltpu.make_async_copy(m_z_out, m_z_in.at[z], m_recv.at[2]).start()

        pl.when(target != f)(away)
        pl.when(target == f)(stay)
    drain(m_z_in, m_recv.at[2])
    drain(z_in, z_recv)
    largest = jnp.max(m_z_in[...], axis=0)
    input_top = jnp.max(largest[0:4], axis=0, keepdims=True)[:, 0:1]
    key_top = jnp.max(largest[4:8], axis=0, keepdims=True)[:, 0:1]
    factor = 36.0 / (input_top * key_top) / math.sqrt(SEQ * FSDP * ULY * TOK)
    raw = z_in[0].astype(jnp.float32)
    for source_z in range(1, SIDE):
        raw += z_in[source_z].astype(jnp.float32)
    out_ref[...] = (raw * factor).astype(jnp.bfloat16)

    for s in range(SEQ):
        drain(qg.at[s, 0:SIDE - 1], q_send.at[s])
        drain(gg.at[s, 0:SIDE - 1], g_send.at[s])
        drain(part_in.at[s], part_send.at[s])
        drain(kg.at[s, 0:ULY - 1], dk_send.at[s])
        drain(dka.at[s, 0], fwd_send.at[s])
    drain(kg.at[:, 0:ULY - 1], kv_send.at[0])
    drain(vg.at[:, 0:ULY - 1], kv_send.at[1])
    drain(xr.at[:, 0, 0:SIDE - 1], x_send.at[0])
    drain(xr.at[:, 1], x_send.at[1])
    for d in range(1, SIDE):
        drain(y_out.at[d - 1], y_send.at[d - 1])
    drain(m_row, m_send.at[0])
    drain(m_y_in, m_send.at[1])

    def drain_last(count):
        drain(z_in.at[0:count], z_send.at[0])
        drain(m_z_in.at[0:count], m_send.at[2])

    pl.when(home == c)(lambda: drain_last(SIDE - 1))
    pl.when(home != c)(lambda: drain_last(SIDE))


def per_device(inputs_norm, queries, key_states, value_states, context_grad):
    bf16, f32 = jnp.bfloat16, jnp.float32
    vmem, dma = pltpu.VMEM, pltpu.SemaphoreType.DMA
    return pl.pallas_call(
        kernel,
        out_shape=jax.ShapeDtypeStruct((OUT_ROWS, COLS), bf16),
        in_specs=[pl.BlockSpec(memory_space=pl.ANY)] * 5,
        out_specs=pl.BlockSpec(memory_space=pltpu.VMEM),
        scratch_shapes=[
            vmem((SEQ, SIDE, TOK, GROUP * HD), bf16),
            vmem((SEQ, SIDE, TOK, GROUP * HD), bf16),
            vmem((SEQ, ULY, TOK, HD), bf16),
            vmem((SEQ, ULY, TOK, HD), bf16),
            vmem((SEQ, 2, SIDE, TOK, BAND), bf16),
            vmem((SEQ, BAND, 2 * SIDE * TOK), bf16),
            vmem((SEQ, SIDE, SIDE, TOK, HD), f32),
            vmem((SEQ, SIDE, SIDE, TOK, HD), bf16),
            vmem((SEQ, SIDE - 1, SIDE, TOK, HD), bf16),
            vmem((SEQ, SIDE, TOK, HD), bf16),
            vmem((SEQ, 2, SIDE, TOK, COLS), bf16),
            vmem((BAND, COLS), f32),
            vmem((SIDE - 1, SLAB, COLS), bf16),
            vmem((SIDE - 1, SLAB, COLS), bf16),
            vmem((SIDE, OUT_ROWS, COLS), bf16),
            vmem((SIDE, OUT_ROWS, COLS), bf16),
            vmem((8, HD), f32),
            vmem((2 * SIDE - 1, 8, HD), f32),
            vmem((8, HD), f32),
            vmem((SIDE - 1, 8, HD), f32),
            vmem((8, HD), f32),
            vmem((SIDE, 8, HD), f32),
            dma((SEQ,)), dma((SEQ,)), dma((2,)), dma, dma((SEQ,)),
            dma((SEQ,)), dma((SEQ,)), dma((SIDE - 1,)), dma, dma((3,)),
            dma((SEQ,)), dma((SEQ,)), dma((2,)), dma((2,)), dma((SEQ,)),
            dma((SEQ,)), dma((SEQ,)), dma((SIDE - 1,)), dma((1,)), dma((3,)),
        ],
        compiler_params=pltpu.CompilerParams(
            collective_id=0, has_side_effects=True, vmem_limit_bytes=56 * 1024 * 1024
        ),
    )(inputs_norm, queries, key_states, value_states, context_grad)


def solution(mesh):
    placed = P(("rep", "fsdp"), "uly", None)
    return jax.shard_map(
        per_device,
        mesh=mesh,
        in_specs=(placed,) * 5,
        out_specs=P(("rep", "uly", "fsdp"), None),
        check_vma=False,
    )
```

time: 587 us -> 89.1 us (0.15)
  blocking collectives: 380 us -> 0 us
  Pallas kernels: 0 us -> 87.5 us
  local copies, waits for them, and re-layouts: 81.8 us -> 1.47 us
  matrix products: 51.1 us -> 0 us
  waiting for transfers between devices: 27.5 us -> 0 us
  starting transfers between devices: 22.9 us -> 0 us
  between operations: 15.2 us -> 0.01 us
    pmax x1 -> x0, blocking collectives: 339 us -> none  [per_device(): input_max, key_max = lax.pmax((input_local, key_local), ('uly', 'fsdp'))]
    pallas_call x0 -> x1, Pallas kernels: none -> 87.5 us  [per_device(): pl.pallas_call(kernel, out_shape=jax.ShapeDtypeStruct((OUT_ROWS, COLS), b...]
    unnamed x34 -> x1, local copies, waits for them, and re-layouts: 52.8 us -> 1.47 us
    all_to_all x2 -> x0, blocking collectives: 40.8 us -> none  [the longest x1 28.3 us: per_device(): lax.all_to_all(inputs_norm, 'uly', split_axis=2, concat_axis=1, tiled=True)]
    dot_general x9 -> x0, matrix products: 33.9 us -> none  [the longest x4 23 us: local_key_grad(): jnp.einsum('hbl,hbd->ld', score_grad, query_block, preferred_element_type...]
    all_to_all x4 -> x0, starting transfers between devices: 22.6 us -> none  [the longest x1 7.58 us: per_device(): lax.all_to_all(key_copies, 'uly', split_axis=2, concat_axis=1, tiled=True)]
    div x4 -> x0, matrix products: 17.1 us -> none  [local_key_grad(): attn_probs = jnp.exp(scores - top_score) / total]
    all_to_all x5 -> x0, local copies, waits for them, and re-layouts: 14.9 us -> none  [the longest x1 10.6 us: per_device(): lax.all_to_all(inputs_norm, 'uly', split_axis=2, concat_axis=1, tiled=True)]
  transfers between devices with their start and end apart: 6 -> 0, of which waited for: 4 -> 0; matrix products, arithmetic and copies ran while one was open for 12% -> 0% of each run, Pallas kernels for 0% -> 0%
where the time goes in v1:
time: 89.1 us; the launch traced here: 89 us
  Pallas kernels  87.5 us (98%)
  local copies, waits for them, and re-layouts  1.47 us (2%)
    pallas_call x1, Pallas kernels, per_device(): pl.pallas_call(kernel, out_shape=jax.ShapeDtypeStruct((OUT_ROWS, COLS), b...  87.5 us

profile of v1, /device:TPU:1, one launch (start us, length us, event | category | flops | bytes accessed | tf_op | source)
XLA Modules:
  0.0 89.0 jit_solution(1422491193589631254)
XLA Ops:
  0.0 87.5 %shard_map.55 = bf16[64,512]{1,0:T(8,128)(2,1)} custom-call(bf16[2,64,8192]{2,1,0:T(8,128)(2,1)} %x_hbm.1, bf16[2,64,4096]{2,1,0:T(8,128)(2,1)} %q_hbm.1, bf16[2,64,512]{2,1,0:T(8,128)(2,1)} %k_hbm.1, bf16[2,64,512]{2,1,0:T(8,128)(2,1)} %v_hbm.1, bf16[2,64,4096]{2,1,0:T(8,128)(2,1)} %g_hbm.1), custom_call_target="tpu_custom_call" | custom-call | tf_op jit(solution)/shard_map/pallas_call | solution.py:312
  87.5 1.5 %copy.7 = bf16[64,512]{1,0:T(8,128)(2,1)} copy(bf16[64,512]{1,0:T(8,128)(2,1)} %shard_map.55) | data formatting | bytes 131072

commit v2 on v1

v2 whole, which is shorter than its diff:
```python
import functools
import math

import jax
import jax.numpy as jnp
from jax import lax
from jax.experimental import pallas as pl
from jax.experimental.pallas import tpu as pltpu
from jax.sharding import PartitionSpec as P

MESH = pl.DeviceIdType.MESH
KVH = 4
HD = 128
SIDE = 4
ULY = SIDE * SIDE
FSDP = 8
SEQ = 2
TOK = 64
GROUP = 8
WIDTH = 8192
BAND = 1024
SLAB = BAND // SIDE
OUT_ROWS = 64
COLS = KVH * HD
PART = 256
SCALE = 1.0 / math.sqrt(HD)
LOG2E = math.log2(math.e)


def kernel(
    x_hbm, q_hbm, k_hbm, v_hbm, g_hbm, out_ref,
    qg, kv, xr, xt, dkacc, part, part_in, dkf, dka, acc,
    y_out, y_in, z_out, z_in, top, m_own, m_row, m_y_out, m_y_in, m_z_out, m_z_in,
    q_recv, kv_recv, kv_all_recv, x_recv, part_recv, dk_recv, y_recv, z_recv, m_recv,
    q_send, kv_send, kv_all_send, x_send, part_send, dk_send, y_send, z_send, m_send,
):
    u = lax.axis_index("uly")
    f = lax.axis_index("fsdp")
    y, x = lax.div(u, SIDE), lax.rem(u, SIDE)
    z, c = lax.div(f, 2), lax.rem(f, 2)
    other = 2 * z + 1 - c
    home = lax.div(f, SIDE)

    def to(du, df):
        return {"uly": du, "fsdp": df}

    def remote(src, dst, send, recv, device):
        return pltpu.make_async_remote_copy(
            src_ref=src, dst_ref=dst, send_sem=send, recv_sem=recv,
            device_id=device, device_id_type=MESH,
        )

    def drain(ref, sem):
        pltpu.make_async_copy(ref, ref, sem).wait()

    def span(start, size):
        return pl.ds(pl.multiple_of(start, size), size)

    def ring(offset):
        return lax.rem(u + offset, ULY)

    place = (x, y)

    def along(axis, offset):
        return lax.rem(place[axis] + offset, SIDE)

    def mate(axis, offset):
        return SIDE * y + along(0, offset) if axis == 0 else SIDE * along(1, offset) + x

    def pick(half, for_first, for_second):
        return jnp.where(half == 0, for_first, for_second)

    barrier = pltpu.get_barrier_semaphore()

    def greet(device):
        pl.semaphore_signal(barrier, inc=1, device_id=device, device_id_type=MESH)

    for d in range(1, ULY):
        greet(to(ring(d), f))
    for d in range(ULY):
        greet(to(ring(d), other))
    for source_z in range(SIDE):
        source = 2 * source_z + home
        pl.when(source != f)(lambda source=source: greet(to(u, source)))

    def kv_here(s):
        return kv.at[:, 0, y] if s == 0 else kv.at[:, 1, :, x]

    def send_heads(s, d):
        target = along(s, d)
        cols = span(target * GROUP * HD, GROUP * HD)
        for which, hbm in enumerate((q_hbm, g_hbm)):
            src, dst = hbm.at[s, :, cols], qg.at[s, place[s], which]
            if d == 0:
                pltpu.make_async_copy(src, dst, q_recv.at[s, d]).start()
            else:
                remote(src, dst, q_send.at[s], q_recv.at[s, d], to(mate(s, d), f)).start()

    def send_kv(s, d):
        cols = span(along(s, d) * HD, HD)
        for which, hbm in enumerate((k_hbm, v_hbm)):
            src, dst = hbm.at[s, :, cols], kv.at[which, s, y, x]
            if d == 0:
                pltpu.make_async_copy(src, dst, kv_recv.at[s]).start()
            else:
                remote(src, dst, kv_send.at[s], kv_recv.at[s], to(mate(s, d), f)).start()

    def send_inputs(same, d):
        half = c if same else 1 - c
        own = pick(half, x, y)
        target = lax.rem(own + d, SIDE)
        device = to(pick(half, mate(0, d), mate(1, d)), 2 * z + half)
        for slab in range(SIDE):
            start = pick(half, (slab * SIDE + target) * 2, (target * SIDE + slab) * 2 + 1)
            src = x_hbm.at[:, :, span(start * SLAB, SLAB)]
            dst = xr.at[:, 0 if same else 1, own, :, pl.ds(slab * SLAB, SLAB)]
            if same and d == 0:
                pltpu.make_async_copy(src, dst, x_recv).start()
            else:
                remote(src, dst, x_send.at[0 if same else 1], x_recv, device).start()

    for s in range(SEQ):
        send_kv(s, 0)
    for s in range(SEQ):
        send_heads(s, 0)
    send_inputs(True, 0)
    pl.semaphore_wait(barrier, 2 * ULY - 1 + SIDE - jnp.where(home == c, 1, 0))
    for s in range(SEQ):
        for d in range(1, SIDE):
            send_kv(s, d)
    for d in range(1, SIDE):
        for s in range(SEQ):
            send_heads(s, d)
    dkacc[...] = jnp.zeros_like(dkacc)
    for s in range(SEQ):
        drain(kv_here(s), kv_recv.at[s])
        for d in range(1, SIDE):
            remote(
                kv_here(s), kv_here(s), kv_all_send.at[s], kv_all_recv.at[s],
                to(mate(1 - s, d), f),
            ).start()
    for d in range(SIDE):
        if d:
            send_inputs(True, d)
        send_inputs(False, d)

    rows = GROUP * TOK
    chunk = SIDE * TOK

    def heads_to_rows(block):
        return jnp.concatenate([block[:, h * HD:(h + 1) * HD] for h in range(GROUP)], axis=0)

    def nt(a, b):
        return lax.dot_general(a, b, (((1,), (1,)), ((), ())), preferred_element_type=jnp.float32)

    def attend_to(s, slot, chunks, block_x):
        query = heads_to_rows(qg[s, slot, 0])
        grad = heads_to_rows(qg[s, slot, 1])
        key_at = lax.broadcasted_iota(jnp.int32, (chunk, rows), 0)
        query_at = lax.rem(lax.broadcasted_iota(jnp.int32, (chunk, rows), 1), TOK)
        scores = []
        for n in range(chunks):
            keys = kv[0, s, n].reshape(chunk, HD)
            scores.append(nt(keys, query) * (SCALE * LOG2E))
        scores[-1] = jnp.where(key_at > query_at + block_x * TOK, -jnp.inf, scores[-1])
        top_score = jnp.max(scores[0], axis=0, keepdims=True)
        for block in scores[1:]:
            top_score = jnp.maximum(top_score, jnp.max(block, axis=0, keepdims=True))
        exps = [jnp.exp2(block - top_score) for block in scores]
        prob_grads = []
        for n in range(chunks):
            values = kv[1, s, n].reshape(chunk, HD)
            prob_grads.append(nt(values, grad))
        total = sum(jnp.sum(e, axis=0, keepdims=True) for e in exps)
        weighted = sum(jnp.sum(e * p, axis=0, keepdims=True) for e, p in zip(exps, prob_grads))
        row_terms = weighted / total
        scale = SCALE / total
        for n in range(chunks):
            score_grad = (exps[n] * ((prob_grads[n] - row_terms) * scale)).astype(jnp.bfloat16)
            term = jnp.dot(score_grad, query, preferred_element_type=jnp.float32)
            dkacc[s, n] += term.reshape(SIDE, TOK, HD)

    def attend(s, d):
        slot = lax.rem(place[s] - d + SIDE, SIDE)
        drain(qg.at[s, slot], q_recv.at[s, d])
        block_y, block_x = (y, slot) if s == 0 else (slot, x)
        for chunks in range(1, SIDE + 1):
            pl.when(block_y == chunks - 1)(
                functools.partial(attend_to, s, slot, chunks, block_x)
            )

    def keys_of(s, index):
        return dkacc[0, index] if s == 0 else dkacc[1, :, index]

    def send_partials(s):
        for index in range(SIDE):
            part[s, index] = keys_of(s, index).astype(jnp.bfloat16)
        for d in range(1, SIDE):
            remote(
                part.at[s, along(1 - s, d)], part_in.at[s, d - 1],
                part_send.at[s], part_recv.at[s], to(mate(1 - s, d), f),
            ).start()

    def send_key_grad(s):
        drain(part_in.at[s], part_recv.at[s])
        summed = keys_of(s, place[1 - s])
        for d in range(SIDE - 1):
            summed += part_in[s, d].astype(jnp.float32)
        dkf[s] = summed.astype(jnp.bfloat16)
        largest = jnp.max(jnp.abs(summed).reshape(SIDE * TOK // 8, 8, HD), axis=0)
        top[...] = largest if s == 0 else jnp.maximum(top[...], largest)
        cols = span(place[s] * HD, HD)

        def copy(half, src, slot, device, here, send):
            dst = dka.at[s, jnp.where(c == half, 0, 1), slot, :, cols]

            def away():
                remote(src, dst, send, dk_recv.at[s], device).start()

            def stay():
                pltpu.make_async_copy(src, dst, dk_recv.at[s]).start()

            if here:
                pl.when(c == half)(stay)
                pl.when(c != half)(away)
            else:
                away()

        for d in range(ULY):
            block = (lax.rem if s == 0 else lax.div)(ring(d), SIDE)
            copy(
                1 - s, dkf.at[s, block], place[1 - s], to(ring(d), 2 * z + 1 - s),
                d == 0, dk_send.at[s, 1],
            )
        for d in range(SIDE):
            copy(
                s, dkf.at[s], slice(None), to(mate(s, d), 2 * z + s), d == 0, dk_send.at[s, 0]
            )

    def grad_rows(s, cols):
        return dka[s, :, :, :, cols].reshape(2 * SIDE * TOK, -1)

    for s in range(SEQ):
        drain(kv.at[:, 0, 0:SIDE - 1] if s == 0 else kv.at[:, 1, :, 0:SIDE - 1], kv_all_recv.at[s])

        def step(d, carry, s=s):
            if s == 1:
                pl.when(d == SIDE - 1)(lambda: send_key_grad(0))
            attend(s, d)
            return carry

        lax.fori_loop(0, SIDE, step, 0)
        send_partials(s)
    send_key_grad(1)

    drain(xr, x_recv)
    input_max = jnp.float32(0.0)
    for s in range(SEQ):
        block = xr[s].reshape(2 * SIDE * TOK, BAND)
        tops = jnp.max(jnp.abs(block), axis=0, keepdims=True).astype(jnp.float32)
        input_max = jnp.maximum(input_max, jnp.max(tops))
        xt[s] = block.T
    key_max = jnp.max(top[...])
    row_at = lax.broadcasted_iota(jnp.int32, (8, HD), 0)
    m_own[...] = jnp.where(row_at < 4, input_max, key_max)
    for dc in range(2):
        for d in range(SIDE):
            if dc or d:
                remote(
                    m_own, m_row.at[dc * SIDE + d - 1], m_send.at[0], m_recv.at[0],
                    to(mate(0, d), f if dc == 0 else other),
                ).start()
    drain(dka.at[0], dk_recv.at[0])
    acc[...] = jnp.dot(xt[0], grad_rows(0, slice(None)), preferred_element_type=jnp.float32)
    drain(m_row, m_recv.at[0])
    m_y_out[...] = jnp.maximum(m_own[...], jnp.max(m_row[...], axis=0))
    for d in range(1, SIDE):
        remote(
            m_y_out, m_y_in.at[d - 1], m_send.at[1], m_recv.at[1], to(mate(1, d), f)
        ).start()
    drain(dka.at[1], dk_recv.at[1])

    own = pick(c, y, x)

    def slab_grad(target, cols):
        at = span(target * SLAB, SLAB)
        return acc[at, cols] + jnp.dot(
            xt[1, at], grad_rows(1, cols), preferred_element_type=jnp.float32
        )

    parts = [slice(p * PART, (p + 1) * PART) for p in range(COLS // PART)]
    for p, cols in enumerate(parts):
        for d in range(1, SIDE):
            y_out[p, d - 1] = slab_grad(lax.rem(own + d, SIDE), cols).astype(jnp.bfloat16)
            remote(
                y_out.at[p, d - 1], y_in.at[p, d - 1], y_send.at[p], y_recv.at[p],
                to(pick(c, mate(1, d), mate(0, d)), f),
            ).start()
    sums = [slab_grad(own, cols) for cols in parts]
    drain(m_y_in, m_recv.at[1])
    m_z_out[...] = jnp.maximum(m_y_out[...], jnp.max(m_y_in[...], axis=0))

    def last_sends(k, src, dst, send, recv):
        target = SIDE * c + k

        def away():
            remote(src, dst, send, recv, to(u, target)).start()

        def stay():
            pltpu.make_async_copy(src, dst, recv).start()

        pl.when(target != f)(away)
        pl.when(target == f)(stay)

    for k in range(SIDE):
        last_sends(k, m_z_out, m_z_in.at[z], m_send.at[2], m_recv.at[2])
    for p in range(len(parts)):
        drain(y_in.at[p], y_recv.at[p])
        for d in range(SIDE - 1):
            sums[p] += y_in[p, d].astype(jnp.float32)
        z_out[p] = sums[p].reshape(SIDE, OUT_ROWS, PART).astype(jnp.bfloat16)
        for k in range(SIDE):
            last_sends(k, z_out.at[p, k], z_in.at[p, z], z_send.at[p], z_recv.at[p])
    drain(m_z_in, m_recv.at[2])
    largest = jnp.max(m_z_in[...], axis=0)
    input_top = jnp.max(largest[0:4], axis=0, keepdims=True)[:, 0:1]
    key_top = jnp.max(largest[4:8], axis=0, keepdims=True)[:, 0:1]
    factor = 36.0 / (input_top * key_top) / math.sqrt(SEQ * FSDP * ULY * TOK)
    for p, cols in enumerate(parts):
        drain(z_in.at[p], z_recv.at[p])
        raw = z_in[p, 0].astype(jnp.float32)
        for source_z in range(1, SIDE):
            raw += z_in[p, source_z].astype(jnp.float32)
        out_ref[:, cols] = (raw * factor).astype(jnp.bfloat16)

    for s in range(SEQ):
        drain(qg.at[s, 0:SIDE - 1], q_send.at[s])
        drain(kv.at[:, s, 0, 0:SIDE - 1], kv_send.at[s])
        drain(kv.at[:, s, 0:SIDE - 1], kv_all_send.at[s])
        drain(part_in.at[s], part_send.at[s])

        def drain_same(s=s):
            drain(part_in.at[s], dk_send.at[s, 0])
            drain(part.at[s], dk_send.at[s, 1])

        def drain_other(s=s):
            drain(part.at[s], dk_send.at[s, 0])
            drain(xt.at[s, 0:(ULY - 1) * TOK * HD // (2 * SIDE * TOK)], dk_send.at[s, 1])

        pl.when(c == s)(drain_same)
        pl.when(c != s)(drain_other)
    drain(xr.at[:, 0, 0:SIDE - 1], x_send.at[0])
    drain(xr.at[:, 1], x_send.at[1])
    for p in range(len(parts)):
        drain(y_in.at[p], y_send.at[p])
    drain(m_row, m_send.at[0])
    drain(m_y_in, m_send.at[1])

    def drain_last(count):
        for p in range(len(parts)):
            drain(z_in.at[p, 0:count], z_send.at[p])
        drain(m_z_in.at[0:count], m_send.at[2])

    pl.when(home == c)(lambda: drain_last(SIDE - 1))
    pl.when(home != c)(lambda: drain_last(SIDE))


def per_device(inputs_norm, queries, key_states, value_states, context_grad):
    bf16, f32 = jnp.bfloat16, jnp.float32
    parts = COLS // PART
    vmem, dma = pltpu.VMEM, pltpu.SemaphoreType.DMA
    return pl.pallas_call(
        kernel,
        out_shape=jax.ShapeDtypeStruct((OUT_ROWS, COLS), bf16),
        in_specs=[pl.BlockSpec(memory_space=pl.ANY)] * 5,
        out_specs=pl.BlockSpec(memory_space=pltpu.VMEM),
        scratch_shapes=[
            vmem((SEQ, SIDE, 2, TOK, GROUP * HD), bf16),
            vmem((2, SEQ, SIDE, SIDE, TOK, HD), bf16),
            vmem((SEQ, 2, SIDE, TOK, BAND), bf16),
            vmem((SEQ, BAND, 2 * SIDE * TOK), bf16),
            vmem((SEQ, SIDE, SIDE, TOK, HD), f32),
            vmem((SEQ, SIDE, SIDE, TOK, HD), bf16),
            vmem((SEQ, SIDE - 1, SIDE, TOK, HD), bf16),
            vmem((SEQ, SIDE, TOK, HD), bf16),
            vmem((SEQ, 2, SIDE, TOK, COLS), bf16),
            vmem((BAND, COLS), f32),
            vmem((parts, SIDE - 1, SLAB, PART), bf16),
            vmem((parts, SIDE - 1, SLAB, PART), bf16),
            vmem((parts, SIDE, OUT_ROWS, PART), bf16),
            vmem((parts, SIDE, OUT_ROWS, PART), bf16),
            vmem((8, HD), f32),
            vmem((8, HD), f32),
            vmem((2 * SIDE - 1, 8, HD), f32),
            vmem((8, HD), f32),
            vmem((SIDE - 1, 8, HD), f32),
            vmem((8, HD), f32),
            vmem((SIDE, 8, HD), f32),
            dma((SEQ, SIDE)), dma((SEQ,)), dma((SEQ,)), dma, dma((SEQ,)),
            dma((SEQ,)), dma((parts,)), dma((parts,)), dma((3,)),
            dma((SEQ,)), dma((SEQ,)), dma((SEQ,)), dma((2,)), dma((SEQ,)),
            dma((SEQ, 2)), dma((parts,)), dma((parts,)), dma((3,)),
        ],
        compiler_params=pltpu.CompilerParams(
            collective_id=0, has_side_effects=True, vmem_limit_bytes=56 * 1024 * 1024
        ),
    )(inputs_norm, queries, key_states, value_states, context_grad)


def solution(mesh):
    placed = P(("rep", "fsdp"), "uly", None)
    return jax.shard_map(
        per_device,
        mesh=mesh,
        in_specs=(placed,) * 5,
        out_specs=P(("rep", "uly", "fsdp"), None),
        check_vma=False,
    )
```

time: 89.1 us -> 77.9 us (0.87)
  Pallas kernels: 87.5 us -> 76.2 us
    pallas_call x1, Pallas kernels: 87.5 us -> 76.2 us  [per_device(): pl.pallas_call(kernel, out_shape=jax.ShapeDtypeStruct((OUT_ROWS, COLS), b...]
where the time goes in v2:
time: 77.9 us; the launch traced here: 77.7 us
  Pallas kernels  76.2 us (98%)
  local copies, waits for them, and re-layouts  1.47 us (2%)
    pallas_call x1, Pallas kernels, per_device(): pl.pallas_call(kernel, out_shape=jax.ShapeDtypeStruct((OUT_ROWS, COLS), b...  76.2 us

profile of v2, /device:TPU:1, one launch (start us, length us, event | category | flops | bytes accessed | tf_op | source)
XLA Modules:
  0.0 77.7 jit_solution(8474974304179304555)
XLA Ops:
  0.0 76.2 %shard_map.55 = bf16[64,512]{1,0:T(8,128)(2,1)} custom-call(bf16[2,64,8192]{2,1,0:T(8,128)(2,1)} %x_hbm.1, bf16[2,64,4096]{2,1,0:T(8,128)(2,1)} %q_hbm.1, bf16[2,64,512]{2,1,0:T(8,128)(2,1)} %k_hbm.1, bf16[2,64,512]{2,1,0:T(8,128)(2,1)} %v_hbm.1, bf16[2,64,4096]{2,1,0:T(8,128)(2,1)} %g_hbm.1), custom_call_target="tpu_custom_call" | custom-call | tf_op jit(solution)/shard_map/pallas_call | solution.py:372
  76.2 1.5 %copy.7 = bf16[64,512]{1,0:T(8,128)(2,1)} copy(bf16[64,512]{1,0:T(8,128)(2,1)} %shard_map.55) | data formatting | bytes 131072

commit v3 on v2

--- a/solution.py
+++ b/solution.py
@@ -22,7 +22,9 @@
 SLAB = BAND // SIDE
 OUT_ROWS = 64
 COLS = KVH * HD
-PART = 256
+INPUTS_AFTER = 0
+GRAD_BEFORE = 0
+PART = 128
 SCALE = 1.0 / math.sqrt(HD)
 LOG2E = math.log2(math.e)
 
@@ -31,8 +33,8 @@
     x_hbm, q_hbm, k_hbm, v_hbm, g_hbm, out_ref,
     qg, kv, xr, xt, dkacc, part, part_in, dkf, dka, acc,
     y_out, y_in, z_out, z_in, top, m_own, m_row, m_y_out, m_y_in, m_z_out, m_z_in,
-    q_recv, kv_recv, kv_all_recv, x_recv, part_recv, dk_recv, y_recv, z_recv, m_recv,
-    q_send, kv_send, kv_all_send, x_send, part_send, dk_send, y_send, z_send, m_send,
+    q_recv, kv_recv, kv_all_recv, x_recv, part_recv, chunk_recv, dk_recv, y_recv, z_recv, m_recv,
+    q_send, kv_send, kv_all_send, x_send, part_send, chunk_send, dk_send, y_send, z_send, m_send,
 ):
     u = lax.axis_index("uly")
     f = lax.axis_index("fsdp")
@@ -125,6 +127,46 @@
         send_heads(s, 0)
     send_inputs(True, 0)
     pl.semaphore_wait(barrier, 2 * ULY - 1 + SIDE - jnp.where(home == c, 1, 0))
+    def share_kv(s):
+        drain(kv_here(s), kv_recv.at[s])
+        for d in range(1, SIDE):
+            def send(d=d):
+                remote(
+                    kv_here(s), kv_here(s), kv_all_send.at[s, d], kv_all_recv.at[s, d],
+                    to(mate(1 - s, d), f),
+                ).start()
+
+            if s == 0:
+                pl.when(y + d < SIDE)(send)
+            else:
+                send()
+
+    def kv_shared(s):
+        for d in range(1, SIDE):
+            def wait(d=d):
+                drain(kv.at[:, s, 0], kv_all_recv.at[s, d])
+
+            if s == 0:
+                pl.when(y >= d)(wait)
+            else:
+                wait()
+
+    def kv_left(s):
+        for d in range(1, SIDE):
+            def wait(d=d):
+                drain(kv.at[:, s, 0], kv_all_send.at[s, d])
+
+            if s == 0:
+                pl.when(y + d < SIDE)(wait)
+            else:
+                wait()
+
+    def send_all_inputs():
+        for d in range(SIDE):
+            if d:
+                send_inputs(True, d)
+            send_inputs(False, d)
+
     for s in range(SEQ):
         for d in range(1, SIDE):
             send_kv(s, d)
@@ -133,16 +175,9 @@
             send_heads(s, d)
     dkacc[...] = jnp.zeros_like(dkacc)
     for s in range(SEQ):
-        drain(kv_here(s), kv_recv.at[s])
-        for d in range(1, SIDE):
-            remote(
-                kv_here(s), kv_here(s), kv_all_send.at[s], kv_all_recv.at[s],
-                to(mate(1 - s, d), f),
-            ).start()
-    for d in range(SIDE):
-        if d:
-            send_inputs(True, d)
-        send_inputs(False, d)
+        share_kv(s)
+    if INPUTS_AFTER < 0:
+        send_all_inputs()
 
     rows = GROUP * TOK
     chunk = SIDE * TOK
@@ -180,78 +215,103 @@
             term = jnp.dot(score_grad, query, preferred_element_type=jnp.float32)
             dkacc[s, n] += term.reshape(SIDE, TOK, HD)
 
-    def attend(s, d):
-        slot = lax.rem(place[s] - d + SIDE, SIDE)
-        drain(qg.at[s, slot], q_recv.at[s, d])
-        block_y, block_x = (y, slot) if s == 0 else (slot, x)
-        for chunks in range(1, SIDE + 1):
-            pl.when(block_y == chunks - 1)(
-                functools.partial(attend_to, s, slot, chunks, block_x)
-            )
-
-    def keys_of(s, index):
-        return dkacc[0, index] if s == 0 else dkacc[1, :, index]
-
-    def send_partials(s):
-        for index in range(SIDE):
-            part[s, index] = keys_of(s, index).astype(jnp.bfloat16)
+    def send_partials():
+        part[0] = dkacc[0].astype(jnp.bfloat16)
         for d in range(1, SIDE):
             remote(
-                part.at[s, along(1 - s, d)], part_in.at[s, d - 1],
-                part_send.at[s], part_recv.at[s], to(mate(1 - s, d), f),
+                part.at[0, along(1, d)], part_in.at[0, d - 1],
+                part_send, part_recv, to(mate(1, d), f),
             ).start()
 
-    def send_key_grad(s):
-        drain(part_in.at[s], part_recv.at[s])
-        summed = keys_of(s, place[1 - s])
+    def send_chunk(n):
+        part[1, :, n] = dkacc[1, n].astype(jnp.bfloat16)
+        for d in range(1, SIDE):
+            remote(
+                part.at[1, along(0, d), n], part_in.at[1, d - 1, n],
+                chunk_send.at[n], chunk_recv.at[n], to(mate(0, d), f),
+            ).start()
+
+    def give(s, half, src, slot, device, here, send):
+        cols = span(place[s] * HD, HD)
+        dst = dka.at[s, jnp.where(c == half, 0, 1), slot, :, cols]
+
+        def away():
+            remote(src, dst, send, dk_recv.at[s], device).start()
+
+        def stay():
+            pltpu.make_async_copy(src, dst, dk_recv.at[s]).start()
+
+        if here is None:
+            away()
+        else:
+            own = jnp.logical_and(here, c == half)
+            pl.when(own)(stay)
+            pl.when(jnp.logical_not(own))(away)
+
+    def widest(summed):
+        return jnp.max(jnp.abs(summed).reshape(-1, 8, HD), axis=0)
+
+    def send_key_grad():
+        drain(part_in.at[0], part_recv)
+        summed = dkacc[0, y]
         for d in range(SIDE - 1):
-            summed += part_in[s, d].astype(jnp.float32)
-        dkf[s] = summed.astype(jnp.bfloat16)
-        largest = jnp.max(jnp.abs(summed).reshape(SIDE * TOK // 8, 8, HD), axis=0)
-        top[...] = largest if s == 0 else jnp.maximum(top[...], largest)
-        cols = span(place[s] * HD, HD)
-
-        def copy(half, src, slot, device, here, send):
-            dst = dka.at[s, jnp.where(c == half, 0, 1), slot, :, cols]
-
-            def away():
-                remote(src, dst, send, dk_recv.at[s], device).start()
-
-            def stay():
-                pltpu.make_async_copy(src, dst, dk_recv.at[s]).start()
-
-            if here:
-                pl.when(c == half)(stay)
-                pl.when(c != half)(away)
-            else:
-                away()
-
+            summed += part_in[0, d].astype(jnp.float32)
+        dkf[0] = summed.astype(jnp.bfloat16)
+        top[...] = widest(summed)
         for d in range(ULY):
-            block = (lax.rem if s == 0 else lax.div)(ring(d), SIDE)
-            copy(
-                1 - s, dkf.at[s, block], place[1 - s], to(ring(d), 2 * z + 1 - s),
-                d == 0, dk_send.at[s, 1],
+            give(
+                0, 1, dkf.at[0, lax.rem(ring(d), SIDE)], y, to(ring(d), 2 * z + 1),
+                True if d == 0 else None, dk_send.at[0, 1],
             )
         for d in range(SIDE):
-            copy(
-                s, dkf.at[s], slice(None), to(mate(s, d), 2 * z + s), d == 0, dk_send.at[s, 0]
+            give(
+                0, 0, dkf.at[0], slice(None), to(mate(0, d), 2 * z),
+                True if d == 0 else None, dk_send.at[0, 0],
+            )
+
+    def send_key_grad_chunk(n):
+        drain(part_in.at[1, 0:SIDE - 1, n], chunk_recv.at[n])
+        summed = dkacc[1, n, x]
+        for d in range(SIDE - 1):
+            summed += part_in[1, d, n].astype(jnp.float32)
+        dkf[1, n] = summed.astype(jnp.bfloat16)
+        top[...] = jnp.maximum(top[...], widest(summed))
+        for d in range(SIDE):
+            give(
+                1, 0, dkf.at[1, n], x, to(SIDE * n + along(0, d), 2 * z),
+                y == n if d == 0 else None, dk_send.at[1, 1],
+            )
+            give(
+                1, 1, dkf.at[1, n], n, to(mate(1, d), 2 * z + 1),
+                True if d == 0 else None, dk_send.at[1, 0],
             )
 
     def grad_rows(s, cols):
         return dka[s, :, :, :, cols].reshape(2 * SIDE * TOK, -1)
 
-    for s in range(SEQ):
-        drain(kv.at[:, 0, 0:SIDE - 1] if s == 0 else kv.at[:, 1, :, 0:SIDE - 1], kv_all_recv.at[s])
-
-        def step(d, carry, s=s):
-            if s == 1:
-                pl.when(d == SIDE - 1)(lambda: send_key_grad(0))
-            attend(s, d)
-            return carry
-
-        lax.fori_loop(0, SIDE, step, 0)
-        send_partials(s)
-    send_key_grad(1)
+    kv_shared(0)
+
+    def step(i, carry):
+        d = i
+        slot = lax.rem(x - d + SIDE, SIDE)
+        drain(qg.at[0, slot], q_recv.at[0, d])
+        for chunks in range(1, SIDE + 1):
+            pl.when(y == chunks - 1)(functools.partial(attend_to, 0, slot, chunks, slot))
+        if INPUTS_AFTER >= 0:
+            pl.when(i == INPUTS_AFTER)(send_all_inputs)
+        return carry
+
+    lax.fori_loop(0, SIDE, step, 0)
+    send_partials()
+    kv_shared(1)
+    for n in reversed(range(SIDE)):
+        drain(qg.at[1, n], q_recv.at[1, lax.rem(y - n + SIDE, SIDE)])
+        attend_to(1, n, n + 1, x)
+        send_chunk(n)
+        if n == GRAD_BEFORE:
+            send_key_grad()
+    for n in reversed(range(SIDE)):
+        send_key_grad_chunk(n)
 
     drain(xr, x_recv)
     input_max = jnp.float32(0.0)
@@ -334,10 +394,7 @@
         out_ref[:, cols] = (raw * factor).astype(jnp.bfloat16)
 
     for s in range(SEQ):
-        drain(qg.at[s, 0:SIDE - 1], q_send.at[s])
         drain(kv.at[:, s, 0, 0:SIDE - 1], kv_send.at[s])
-        drain(kv.at[:, s, 0:SIDE - 1], kv_all_send.at[s])
-        drain(part_in.at[s], part_send.at[s])
 
         def drain_same(s=s):
             drain(part_in.at[s], dk_send.at[s, 0])
@@ -349,6 +406,13 @@
 
         pl.when(c == s)(drain_same)
         pl.when(c != s)(drain_other)
+    drain(qg.at[1, 0:SIDE - 1], q_send.at[1])
+    kv_left(1)
+    drain(part_in.at[0], part_send)
+    drain(qg.at[0, 0:SIDE - 1], q_send.at[0])
+    kv_left(0)
+    for n in range(SIDE):
+        drain(part_in.at[1, 0:SIDE - 1, n], chunk_send.at[n])
     drain(xr.at[:, 0, 0:SIDE - 1], x_send.at[0])
     drain(xr.at[:, 1], x_send.at[1])
     for p in range(len(parts)):
@@ -396,9 +460,9 @@
             vmem((SIDE - 1, 8, HD), f32),
             vmem((8, HD), f32),
             vmem((SIDE, 8, HD), f32),
-            dma((SEQ, SIDE)), dma((SEQ,)), dma((SEQ,)), dma, dma((SEQ,)),
+            dma((SEQ, SIDE)), dma((SEQ,)), dma((SEQ, SIDE)), dma, dma, dma((SIDE,)),
             dma((SEQ,)), dma((parts,)), dma((parts,)), dma((3,)),
-            dma((SEQ,)), dma((SEQ,)), dma((SEQ,)), dma((2,)), dma((SEQ,)),
+            dma((SEQ,)), dma((SEQ,)), dma((SEQ, SIDE)), dma((2,)), dma, dma((SIDE,)),
             dma((SEQ, 2)), dma((parts,)), dma((parts,)), dma((3,)),
         ],
         compiler_params=pltpu.CompilerParams(

time: 77.9 us -> 76.1 us (0.977)
  Pallas kernels: 76.2 us -> 74.4 us
    pallas_call x1, Pallas kernels: 76.2 us -> 74.4 us  [per_device(): pl.pallas_call(kernel, out_shape=jax.ShapeDtypeStruct((OUT_ROWS, COLS), b...]
where the time goes in v3:
time: 76.1 us; the launch traced here: 75.9 us
  Pallas kernels  74.4 us (98%)
  local copies, waits for them, and re-layouts  1.47 us (2%)
    pallas_call x1, Pallas kernels, per_device(): pl.pallas_call(kernel, out_shape=jax.ShapeDtypeStruct((OUT_ROWS, COLS), b...  74.4 us

profile of v3, /device:TPU:1, one launch (start us, length us, event | category | flops | bytes accessed | tf_op | source)
XLA Modules:
  0.0 75.9 jit_solution(16859646317091667614)
XLA Ops:
  0.0 74.4 %shard_map.55 = bf16[64,512]{1,0:T(8,128)(2,1)} custom-call(bf16[2,64,8192]{2,1,0:T(8,128)(2,1)} %x_hbm.1, bf16[2,64,4096]{2,1,0:T(8,128)(2,1)} %q_hbm.1, bf16[2,64,512]{2,1,0:T(8,128)(2,1)} %k_hbm.1, bf16[2,64,512]{2,1,0:T(8,128)(2,1)} %v_hbm.1, bf16[2,64,4096]{2,1,0:T(8,128)(2,1)} %g_hbm.1), custom_call_target="tpu_custom_call" | custom-call | tf_op jit(solution)/shard_map/pallas_call | solution.py:436
  74.4 1.5 %copy.7 = bf16[64,512]{1,0:T(8,128)(2,1)} copy(bf16[64,512]{1,0:T(8,128)(2,1)} %shard_map.55) | data formatting | bytes 131072

commit v4 on v3

--- a/solution.py
+++ b/solution.py
@@ -22,8 +22,11 @@
 SLAB = BAND // SIDE
 OUT_ROWS = 64
 COLS = KVH * HD
+EARLY = (0, 1)
+HEADS = (1, 2, 3)
 INPUTS_AFTER = 0
-GRAD_BEFORE = 0
+GRAD_AFTER = 2
+FAR_FIRST = (2, 1, 3)
 PART = 128
 SCALE = 1.0 / math.sqrt(HD)
 LOG2E = math.log2(math.e)
@@ -129,7 +132,7 @@
     pl.semaphore_wait(barrier, 2 * ULY - 1 + SIDE - jnp.where(home == c, 1, 0))
     def share_kv(s):
         drain(kv_here(s), kv_recv.at[s])
-        for d in range(1, SIDE):
+        for d in FAR_FIRST:
             def send(d=d):
                 remote(
                     kv_here(s), kv_here(s), kv_all_send.at[s, d], kv_all_recv.at[s, d],
@@ -161,23 +164,23 @@
             else:
                 wait()
 
-    def send_all_inputs():
-        for d in range(SIDE):
+    def send_all_inputs(offsets):
+        for d in offsets:
             if d:
                 send_inputs(True, d)
             send_inputs(False, d)
 
     for s in range(SEQ):
-        for d in range(1, SIDE):
+        for d in FAR_FIRST:
             send_kv(s, d)
-    for d in range(1, SIDE):
+    for d in HEADS:
         for s in range(SEQ):
             send_heads(s, d)
     dkacc[...] = jnp.zeros_like(dkacc)
+    top[...] = jnp.zeros_like(top)
     for s in range(SEQ):
         share_kv(s)
-    if INPUTS_AFTER < 0:
-        send_all_inputs()
+    send_all_inputs(EARLY)
 
     rows = GROUP * TOK
     chunk = SIDE * TOK
@@ -217,7 +220,7 @@
 
     def send_partials():
         part[0] = dkacc[0].astype(jnp.bfloat16)
-        for d in range(1, SIDE):
+        for d in FAR_FIRST:
             remote(
                 part.at[0, along(1, d)], part_in.at[0, d - 1],
                 part_send, part_recv, to(mate(1, d), f),
@@ -225,7 +228,7 @@
 
     def send_chunk(n):
         part[1, :, n] = dkacc[1, n].astype(jnp.bfloat16)
-        for d in range(1, SIDE):
+        for d in FAR_FIRST:
             remote(
                 part.at[1, along(0, d), n], part_in.at[1, d - 1, n],
                 chunk_send.at[n], chunk_recv.at[n], to(mate(0, d), f),
@@ -257,13 +260,13 @@
         for d in range(SIDE - 1):
             summed += part_in[0, d].astype(jnp.float32)
         dkf[0] = summed.astype(jnp.bfloat16)
-        top[...] = widest(summed)
-        for d in range(ULY):
+        top[...] = jnp.maximum(top[...], widest(summed))
+        for d in (10, 6, 9, 11, 14, 2, 8, 5, 7, 13, 15, 1, 3, 4, 12, 0):
             give(
                 0, 1, dkf.at[0, lax.rem(ring(d), SIDE)], y, to(ring(d), 2 * z + 1),
                 True if d == 0 else None, dk_send.at[0, 1],
             )
-        for d in range(SIDE):
+        for d in (*FAR_FIRST, 0):
             give(
                 0, 0, dkf.at[0], slice(None), to(mate(0, d), 2 * z),
                 True if d == 0 else None, dk_send.at[0, 0],
@@ -276,7 +279,7 @@
             summed += part_in[1, d, n].astype(jnp.float32)
         dkf[1, n] = summed.astype(jnp.bfloat16)
         top[...] = jnp.maximum(top[...], widest(summed))
-        for d in range(SIDE):
+        for d in (*FAR_FIRST, 0):
             give(
                 1, 0, dkf.at[1, n], x, to(SIDE * n + along(0, d), 2 * z),
                 y == n if d == 0 else None, dk_send.at[1, 1],
@@ -297,8 +300,8 @@
         drain(qg.at[0, slot], q_recv.at[0, d])
         for chunks in range(1, SIDE + 1):
             pl.when(y == chunks - 1)(functools.partial(attend_to, 0, slot, chunks, slot))
-        if INPUTS_AFTER >= 0:
-            pl.when(i == INPUTS_AFTER)(send_all_inputs)
+        late = [d for d in range(SIDE) if d not in EARLY]
+        pl.when(i == INPUTS_AFTER)(lambda: send_all_inputs(late))
         return carry
 
     lax.fori_loop(0, SIDE, step, 0)
@@ -308,10 +311,10 @@
         drain(qg.at[1, n], q_recv.at[1, lax.rem(y - n + SIDE, SIDE)])
         attend_to(1, n, n + 1, x)
         send_chunk(n)
-        if n == GRAD_BEFORE:
-            send_key_grad()
     for n in reversed(range(SIDE)):
         send_key_grad_chunk(n)
+        if n == GRAD_AFTER:
+            send_key_grad()
 
     drain(xr, x_recv)
     input_max = jnp.float32(0.0)
@@ -350,7 +353,7 @@
 
     parts = [slice(p * PART, (p + 1) * PART) for p in range(COLS // PART)]
     for p, cols in enumerate(parts):
-        for d in range(1, SIDE):
+        for d in FAR_FIRST:
             y_out[p, d - 1] = slab_grad(lax.rem(own + d, SIDE), cols).astype(jnp.bfloat16)
             remote(
                 y_out.at[p, d - 1], y_in.at[p, d - 1], y_send.at[p], y_recv.at[p],

time: 76.1 us -> 74.7 us (0.982)
  Pallas kernels: 74.4 us -> 73 us
    pallas_call x1, Pallas kernels: 74.4 us -> 73 us  [per_device(): pl.pallas_call(kernel, out_shape=jax.ShapeDtypeStruct((OUT_ROWS, COLS), b...]
where the time goes in v4:
time: 74.7 us; the launch traced here: 74.5 us
  Pallas kernels  73 us (98%)
  local copies, waits for them, and re-layouts  1.47 us (2%)
    pallas_call x1, Pallas kernels, per_device(): pl.pallas_call(kernel, out_shape=jax.ShapeDtypeStruct((OUT_ROWS, COLS), b...  73 us

profile of v4, /device:TPU:1, one launch (start us, length us, event | category | flops | bytes accessed | tf_op | source)
XLA Modules:
  0.0 74.5 jit_solution(7321386073067374544)
XLA Ops:
  0.0 73.0 %shard_map.55 = bf16[64,512]{1,0:T(8,128)(2,1)} custom-call(bf16[2,64,8192]{2,1,0:T(8,128)(2,1)} %x_hbm.1, bf16[2,64,4096]{2,1,0:T(8,128)(2,1)} %q_hbm.1, bf16[2,64,512]{2,1,0:T(8,128)(2,1)} %k_hbm.1, bf16[2,64,512]{2,1,0:T(8,128)(2,1)} %v_hbm.1, bf16[2,64,4096]{2,1,0:T(8,128)(2,1)} %g_hbm.1), custom_call_target="tpu_custom_call" | custom-call | tf_op jit(solution)/shard_map/pallas_call | solution.py:439
  73.0 1.5 %copy.7 = bf16[64,512]{1,0:T(8,128)(2,1)} copy(bf16[64,512]{1,0:T(8,128)(2,1)} %shard_map.55) | data formatting | bytes 131072

commit v5 on v4

--- a/solution.py
+++ b/solution.py
@@ -22,7 +22,7 @@
 SLAB = BAND // SIDE
 OUT_ROWS = 64
 COLS = KVH * HD
-EARLY = (0, 1)
+EARLY = (0, 1, 3)
 HEADS = (1, 2, 3)
 INPUTS_AFTER = 0
 GRAD_AFTER = 2

time: 74.7 us -> 72.2 us (0.967)
  Pallas kernels: 73 us -> 70.6 us
    pallas_call x1, Pallas kernels: 73 us -> 70.6 us  [per_device(): pl.pallas_call(kernel, out_shape=jax.ShapeDtypeStruct((OUT_ROWS, COLS), b...]
where the time goes in v5:
time: 72.2 us; the launch traced here: 72.1 us
  Pallas kernels  70.6 us (98%)
  local copies, waits for them, and re-layouts  1.47 us (2%)
    pallas_call x1, Pallas kernels, per_device(): pl.pallas_call(kernel, out_shape=jax.ShapeDtypeStruct((OUT_ROWS, COLS), b...  70.6 us
    unnamed x1, local copies, waits for them, and re-layouts  1.47 us

profile of v5, /device:TPU:1, one launch (start us, length us, event | category | flops | bytes accessed | tf_op | source)
XLA Modules:
  0.0 72.1 jit_solution(2272251099159792522)
XLA Ops:
  0.0 70.6 %shard_map.55 = bf16[64,512]{1,0:T(8,128)(2,1)} custom-call(bf16[2,64,8192]{2,1,0:T(8,128)(2,1)} %x_hbm.1, bf16[2,64,4096]{2,1,0:T(8,128)(2,1)} %q_hbm.1, bf16[2,64,512]{2,1,0:T(8,128)(2,1)} %k_hbm.1, bf16[2,64,512]{2,1,0:T(8,128)(2,1)} %v_hbm.1, bf16[2,64,4096]{2,1,0:T(8,128)(2,1)} %g_hbm.1), custom_call_target="tpu_custom_call" | custom-call | tf_op jit(solution)/shard_map/pallas_call | solution.py:439
  70.6 1.5 %copy.7 = bf16[64,512]{1,0:T(8,128)(2,1)} copy(bf16[64,512]{1,0:T(8,128)(2,1)} %shard_map.55) | data formatting | bytes 131072
